TPU v7x, 32 devices: a whole 2x2x4 slice. The times are simulated.
32 devices in a mesh: dp: 16 (over z, y, core), tensor: 2 (over x).
Axes of the slice: x: 2, y: 2, z: 4, core: 2. Of those that a mesh axis runs over, the one named last changes fastest.
Arguments:
- hidden_in: bfloat16 [16384, 1024], P(('dp', 'tensor')), may hold values from -6 to 6
- memory: bfloat16 [16384, 1024], P(('dp', 'tensor')), may hold values from -6 to 6
- in_proj: bfloat16 [2, 3, 1024, 1024], P(None, None, 'tensor'), may hold values from -0.1875 to 0.1875
- in_bias: float32 [2, 2, 1024], P(None, None, 'tensor'), may hold values from -1.8 to 1.8
- out_proj: bfloat16 [2, 1024, 1024], P(None, 'tensor'), may hold values from -1.5 to 1.5
- ffn_up: bfloat16 [4096, 1024], P('tensor'), may hold values from -0.1875 to 0.1875
- ffn_up_bias: float32 [4096], P('tensor'), may hold values from -1.8 to 1.8
- ffn_down: bfloat16 [4096, 1024], P('tensor'), may hold values from -0.09375 to 0.09375
- out_bias: float32 [3, 1024], replicated, may hold values from -1.8 to 1.8
- norm_gain: float32 [3, 1024], replicated, may hold values from 0.5 to 1.5
- norm_bias: float32 [3, 1024], replicated, may hold values from -1.8 to 1.8
- out_grad: bfloat16 [16384, 1024], P(('dp', 'tensor')), may hold values from -6 to 6
- target_len: int32 [16], replicated, may hold values from 1 to 1024, 10240 in all
- source_len: int32 [16], replicated, may hold values from 1 to 1024, 10240 in all
- assignment: int32 [16], P('dp'), may hold values from 0 to 15, each once
Outputs:
- hidden_out: bfloat16 [16384, 1024], P(('dp', 'tensor'))
- hidden_grad: float32 [16384, 1024], P(('dp', 'tensor'))
- memory_grad: float32 [16384, 1024], P(('dp', 'tensor'))
- in_proj_grad: float32 [2, 3, 1024, 1024], P(None, None, 'tensor', 'dp')
- out_proj_grad: float32 [2, 1024, 1024], P(None, 'tensor', 'dp')
- ffn_up_grad: float32 [4096, 1024], P('tensor', 'dp')
- ffn_down_grad: float32 [4096, 1024], P('tensor', 'dp')
- in_bias_grad: float32 [2, 2, 1024], replicated
- ffn_up_bias_grad: float32 [4096], replicated
- out_bias_grad: float32 [3, 1024], replicated
- norm_gain_grad: float32 [3, 1024], replicated
- norm_bias_grad: float32 [3, 1024], replicated
Inputs may be any that keep to these rules, and one draw needn't show every extreme that they name: `target_len`: each row's target length; the longest is 1024. `source_len`: each row's memory length; the longest is 1024. `assignment`: a permutation of the 16 rows.
All inputs are finite; a program needn't handle non-finite values.
Results may differ from a plain program's by a relative error of at most 0.018.
Values may be sent and summed in bfloat16 or wider, within the bound.
No kernel may reach another device: no remote copies, remote signals or barrier semaphores. Data moves between devices by JAX's collectives and lax.ppermute only.
A program may use at most 320 MiB of HBM per device.

v0:
```python
import jax
import jax.numpy as jnp
from jax import lax
from jax.sharding import PartitionSpec as P

D = 1024
HEAD_DIM = 64
FF = 4096


epsilon = 1e-05
masked_score = -1e30
root_half = 0.7071067811865476
normal_peak = 0.3989422804014327


def normalize(values, gain_row, shift_row):
    centred = values - jnp.mean(values, axis=-1, keepdims=True)
    inverse = lax.rsqrt(jnp.mean(centred * centred, axis=-1, keepdims=True) + epsilon)
    unit_rows = centred * inverse
    return (unit_rows * gain_row + shift_row, unit_rows, inverse)


def normalize_back(gradient, unit_rows, inverse, gain_row):
    scaled = gradient * gain_row
    return inverse * (
        scaled
        - jnp.mean(scaled, axis=-1, keepdims=True)
        - unit_rows * jnp.mean(scaled * unit_rows, axis=-1, keepdims=True)
    )


def gelu_slope(values):
    return (
        0.5 * (1.0 + lax.erf(values * root_half))
        + values * jnp.exp(-0.5 * values * values) * normal_peak
    )


def project(matrix, weight):
    return lax.dot_general(
        matrix, weight, (((1,), (1,)), ((), ())), preferred_element_type=jnp.float32
    )


def outer_sum(left_mat, right_mat):
    return lax.dot_general(
        left_mat, right_mat, (((0,), (0,)), ((), ())), preferred_element_type=jnp.float32
    )


def apply_right(matrix, weight):
    return jnp.dot(matrix, weight, preferred_element_type=jnp.float32)


def allowed_keys(length, first_row, query_count, key_count, causal):
    key_pos = lax.iota(jnp.int32, key_count)[None, :]
    allowed = jnp.broadcast_to(key_pos < length, (query_count, key_count))
    if causal:
        query_pos = first_row + lax.iota(jnp.int32, query_count)[:, None]
        allowed = allowed & (key_pos <= query_pos)
    return allowed


def masked_scores(query, keys, allowed):
    scores = jnp.einsum(
        "qhe,khe->hqk", query, keys, preferred_element_type=jnp.float32
    ) * HEAD_DIM ** (-0.5)
    return jnp.where(allowed[None], scores, masked_score)


def attend_forward(query, keys, values, lengths, causal):
    slot_count = lengths.shape[0]
    query_len = query.shape[0] // slot_count
    key_len = keys.shape[0] // slot_count
    block_rows = min(512, query_len)
    outputs = []
    log_sums = []
    key_slot = keys.reshape(key_len, -1, HEAD_DIM)
    value_slot = values.reshape(key_len, -1, HEAD_DIM)
    for first_row in range(0, query_len, block_rows):
        query_block = query[first_row : first_row + block_rows].reshape(block_rows, -1, HEAD_DIM)
        allowed = allowed_keys(lengths[0], first_row, block_rows, key_len, causal)
        scores = masked_scores(query_block, key_slot, allowed)
        row_max = jnp.max(scores, axis=-1, keepdims=True)
        exp_scores = jnp.exp(scores - row_max)
        row_total = jnp.sum(exp_scores, axis=-1, keepdims=True)
        attn_probs = (exp_scores / row_total).astype(jnp.bfloat16)
        mixed = jnp.einsum(
            "hqk,khe->qhe", attn_probs, value_slot, preferred_element_type=jnp.float32
        )
        outputs.append(mixed.reshape(block_rows, -1))
        log_sums.append(row_max + jnp.log(row_total))
    return (jnp.concatenate(outputs, axis=0).astype(jnp.bfloat16), log_sums)


def attend_backward(query, keys, values, lengths, causal, log_sums, grad_mixed):
    slot_count = lengths.shape[0]
    query_len = query.shape[0] // slot_count
    key_len = keys.shape[0] // slot_count
    block_rows = min(512, query_len)
    score_scale = HEAD_DIM ** (-0.5)
    query_grads = []
    block_index = 0
    key_slot = keys.reshape(key_len, -1, HEAD_DIM)
    value_slot = values.reshape(key_len, -1, HEAD_DIM)
    key_acc = jnp.zeros(key_slot.shape, jnp.float32)
    value_acc = jnp.zeros(value_slot.shape, jnp.float32)
    for first_row in range(0, query_len, block_rows):
        query_block = query[first_row : first_row + block_rows].reshape(block_rows, -1, HEAD_DIM)
        grad_block = grad_mixed[first_row : first_row + block_rows].reshape(
            block_rows, -1, HEAD_DIM
        )
        allowed = allowed_keys(lengths[0], first_row, block_rows, key_len, causal)
        scores = masked_scores(query_block, key_slot, allowed)
        attn_probs = jnp.exp(scores - log_sums[block_index])
        block_index += 1
        grad_probs = jnp.einsum(
            "qhe,khe->hqk", grad_block, value_slot, preferred_element_type=jnp.float32
        )
        row_delta = jnp.sum(attn_probs * grad_probs, axis=-1, keepdims=True)
        grad_scores = (attn_probs * (grad_probs - row_delta)).astype(jnp.bfloat16)
        grad_query = (
            jnp.einsum("hqk,khe->qhe", grad_scores, key_slot, preferred_element_type=jnp.float32)
            * score_scale
        )
        query_grads.append(grad_query.astype(jnp.bfloat16).reshape(block_rows, -1))
        key_acc = key_acc + jnp.einsum(
            "hqk,qhe->khe", grad_scores, query_block, preferred_element_type=jnp.float32
        )
        value_acc = value_acc + jnp.einsum(
            "hqk,qhe->khe",
            attn_probs.astype(jnp.bfloat16),
            grad_block,
            preferred_element_type=jnp.float32,
        )
    key_grads = (key_acc * score_scale).astype(jnp.bfloat16).reshape(key_len, -1)
    value_grads = value_acc.astype(jnp.bfloat16).reshape(key_len, -1)
    return (jnp.concatenate(query_grads, axis=0), key_grads, value_grads)


def branch_total(branch_part):
    return lax.psum_scatter(branch_part, "tensor", scatter_dimension=0, tiled=True)


def gather_normed(normed):
    return lax.all_gather(normed, "tensor", axis=0, tiled=True)


def gather_grads(gradient):
    return lax.all_gather(gradient, "tensor", axis=0, tiled=True)


def input_total(branch_part):
    return lax.psum_scatter(branch_part, "tensor", scatter_dimension=0, tiled=True)


def shards(
    hidden_in,
    memory,
    in_proj,
    in_bias,
    out_proj,
    ffn_up,
    ffn_up_bias,
    ffn_down,
    out_bias,
    norm_gain,
    norm_bias,
    out_grad,
    target_len,
    source_len,
    assignment,
):
    row_count = target_len.shape[0]
    owner_mask = assignment[:, None] == lax.iota(jnp.int32, row_count)[None, :]
    target_lengths = jnp.sum(jnp.where(owner_mask, target_len[None, :], 0), axis=1)
    source_lengths = jnp.sum(jnp.where(owner_mask, source_len[None, :], 0), axis=1)
    stream_zero = hidden_in.astype(jnp.float32)
    normed_one, unit_one, inverse_one = normalize(stream_zero, norm_gain[0], norm_bias[0])
    rows_one, memory_rows = (
        lax.all_gather(normed_one.astype(jnp.bfloat16), "tensor", axis=0, tiled=True),
        lax.all_gather(memory, "tensor", axis=0, tiled=True),
    )
    self_proj = jnp.einsum("nd,cfd->cnf", rows_one, in_proj[0], preferred_element_type=jnp.float32)
    query_one = (self_proj[0] + in_bias[0, 0]).astype(jnp.bfloat16)
    key_one = self_proj[1].astype(jnp.bfloat16)
    value_one = (self_proj[2] + in_bias[0, 1]).astype(jnp.bfloat16)
    mixed_one, sums_one = attend_forward(query_one, key_one, value_one, target_lengths, True)
    stream_one = stream_zero + branch_total(apply_right(mixed_one, out_proj[0])) + out_bias[0]
    normed_two, unit_two, inverse_two = normalize(stream_one, norm_gain[1], norm_bias[1])
    rows_two = gather_normed(normed_two.astype(jnp.bfloat16))
    query_two = (project(rows_two, in_proj[1, 0]) + in_bias[1, 0]).astype(jnp.bfloat16)
    memory_proj = jnp.einsum(
        "nd,cfd->cnf", memory_rows, in_proj[1, 1:], preferred_element_type=jnp.float32
    )
    key_two = memory_proj[0].astype(jnp.bfloat16)
    value_two = (memory_proj[1] + in_bias[1, 1]).astype(jnp.bfloat16)
    mixed_two, sums_two = attend_forward(query_two, key_two, value_two, source_lengths, False)
    stream_two = stream_one + branch_total(apply_right(mixed_two, out_proj[1])) + out_bias[1]
    normed_three, unit_three, inverse_three = normalize(stream_two, norm_gain[2], norm_bias[2])
    rows_three = gather_normed(normed_three.astype(jnp.bfloat16))
    pre_active = project(rows_three, ffn_up) + ffn_up_bias
    active = jax.nn.gelu(pre_active, approximate=False).astype(jnp.bfloat16)
    hidden_out = (stream_two + branch_total(apply_right(active, ffn_down)) + out_bias[2]).astype(
        jnp.bfloat16
    )
    grad_stream = out_grad.astype(jnp.float32)
    down_three = gather_grads(out_grad)
    unit_slope = gelu_slope(pre_active)
    grad_down = outer_sum(active, down_three)
    grad_active = project(down_three, ffn_down).astype(jnp.bfloat16)
    grad_pre = (grad_active.astype(jnp.float32) * unit_slope).astype(jnp.bfloat16)
    grad_up = outer_sum(grad_pre, rows_three)
    grad_up_bias = jnp.sum(grad_pre.astype(jnp.float32), axis=0)
    back_three = input_total(apply_right(grad_pre, ffn_up))
    grad_two = grad_stream + normalize_back(back_three, unit_three, inverse_three, norm_gain[2])
    down_two = gather_grads(grad_two.astype(jnp.bfloat16))
    grad_out_two = outer_sum(mixed_two, down_two)
    grad_mixed_two = project(down_two, out_proj[1]).astype(jnp.bfloat16)
    grad_query_two, grad_key_two, grad_value_two = attend_backward(
        query_two, key_two, value_two, source_lengths, False, sums_two, grad_mixed_two
    )
    grad_in_two = jnp.stack(
        [
            outer_sum(grad_query_two, rows_two),
            outer_sum(grad_key_two, memory_rows),
            outer_sum(grad_value_two, memory_rows),
        ]
    )
    bias_two = jnp.stack(
        [
            jnp.sum(grad_query_two.astype(jnp.float32), axis=0),
            jnp.sum(grad_value_two.astype(jnp.float32), axis=0),
        ]
    )
    memory_part = apply_right(grad_key_two, in_proj[1, 1]) + apply_right(
        grad_value_two, in_proj[1, 2]
    )
    back_two, memory_grad = (
        lax.psum_scatter(
            apply_right(grad_query_two, in_proj[1, 0]), "tensor", scatter_dimension=0, tiled=True
        ),
        lax.psum_scatter(memory_part, "tensor", scatter_dimension=0, tiled=True),
    )
    grad_one = grad_two + normalize_back(back_two, unit_two, inverse_two, norm_gain[1])
    down_one = gather_grads(grad_one.astype(jnp.bfloat16))
    grad_out_one = outer_sum(mixed_one, down_one)
    grad_mixed_one = project(down_one, out_proj[0]).astype(jnp.bfloat16)
    grad_query_one, grad_key_one, grad_value_one = attend_backward(
        query_one, key_one, value_one, target_lengths, True, sums_one, grad_mixed_one
    )
    grad_stack = jnp.stack([grad_query_one, grad_key_one, grad_value_one])
    grad_in_one = jnp.einsum(
        "cnf,nd->cfd", grad_stack, rows_one, preferred_element_type=jnp.float32
    )
    bias_one = jnp.stack(
        [
            jnp.sum(grad_query_one.astype(jnp.float32), axis=0),
            jnp.sum(grad_value_one.astype(jnp.float32), axis=0),
        ]
    )
    back_one = input_total(
        jnp.einsum("cnf,cfd->nd", grad_stack, in_proj[0], preferred_element_type=jnp.float32)
    )
    hidden_grad = grad_one + normalize_back(back_one, unit_one, inverse_one, norm_gain[0])
    in_shares, out_shares, up_share, down_share = (
        lax.psum_scatter(
            jnp.stack([grad_in_one, grad_in_two]).reshape(-1, D),
            "dp",
            scatter_dimension=1,
            tiled=True,
        ),
        lax.psum_scatter(
            jnp.stack([grad_out_one, grad_out_two]).reshape(-1, D),
            "dp",
            scatter_dimension=1,
            tiled=True,
        ),
        lax.psum_scatter(grad_up, "dp", scatter_dimension=1, tiled=True),
        lax.psum_scatter(grad_down, "dp", scatter_dimension=1, tiled=True),
    )
    in_proj_grad = in_shares.reshape(2, 3, -1, in_shares.shape[-1])
    out_proj_grad = out_shares.reshape(2, -1, out_shares.shape[-1])
    tensor_part = lax.axis_index("tensor")
    head_width = in_bias.shape[-1]
    bias_full = lax.dynamic_update_slice(
        jnp.zeros((2, 2, D), jnp.float32),
        jnp.stack([bias_one, bias_two]),
        (jnp.int32(0), jnp.int32(0), tensor_part * head_width),
    )
    up_bias_full = lax.dynamic_update_slice(
        jnp.zeros((FF,), jnp.float32), grad_up_bias, (tensor_part * grad_up_bias.shape[0],)
    )
    out_bias_terms = jnp.stack(
        [jnp.sum(grad_one, axis=0), jnp.sum(grad_two, axis=0), jnp.sum(grad_stream, axis=0)]
    )
    gain_terms = jnp.stack(
        [
            jnp.sum(back_one * unit_one, axis=0),
            jnp.sum(back_two * unit_two, axis=0),
            jnp.sum(back_three * unit_three, axis=0),
        ]
    )
    shift_terms = jnp.stack(
        [jnp.sum(back_one, axis=0), jnp.sum(back_two, axis=0), jnp.sum(back_three, axis=0)]
    )
    in_bias_grad, ffn_up_bias_grad, out_bias_grad, norm_gain_grad, norm_bias_grad = lax.psum(
        (bias_full, up_bias_full, out_bias_terms, gain_terms, shift_terms), ("dp", "tensor")
    )
    return (
        hidden_out,
        hidden_grad,
        memory_grad,
        in_proj_grad,
        out_proj_grad,
        up_share,
        down_share,
        in_bias_grad,
        ffn_up_bias_grad,
        out_bias_grad,
        norm_gain_grad,
        norm_bias_grad,
    )


def solution(mesh):
    return jax.shard_map(
        shards,
        mesh=mesh,
        in_specs=(
            P(("dp", "tensor"), None),
            P(("dp", "tensor"), None),
            P(None, None, "tensor", None),
            P(None, None, "tensor"),
            P(None, "tensor", None),
            P("tensor", None),
            P("tensor"),
            P("tensor", None),
            P(),
            P(),
            P(),
            P(("dp", "tensor"), None),
            P(),
            P(),
            P("dp"),
        ),
        out_specs=(
            P(("dp", "tensor"), None),
            P(("dp", "tensor"), None),
            P(("dp", "tensor"), None),
            P(None, None, "tensor", "dp"),
            P(None, "tensor", "dp"),
            P("tensor", "dp"),
            P("tensor", "dp"),
            P(),
            P(),
            P(),
            P(),
            P(),
        ),
        check_vma=False,
    )
```

profile of v0, /device:TPU:8, one launch (start us, length us, event | category | flops | bytes accessed | tf_op | source)
XLA Modules:
  0.0 1440.2 jit_solution(2365456156968368112)
XLA Ops:
  17.4 31.8 %all-gather.8.cloned.1.call-done = bf16[1024,1024]{1,0:T(8,128)(2,1)} async-done(((bf16[512,1024]{1,0:T(8,128)(2,1)}), bf16[1024,1024]{1,0:T(8,128)(2,1)}) %all-gather.8.cloned.1.call-update) | async-done | bytes 2097168 | tf_op jit(solution)/shard_map/all_gather | solution.py:182
  88.0 53.0 %reduce-scatter.12.cloned.1.call-done = f32[512,1024]{1,0:T(8,128)} async-done(((f32[1024,1024]{1,0:T(8,128)}), f32[512,1024]{1,0:T(8,128)}) %reduce-scatter.12.cloned.1.call-update) | async-done | bytes 2097168 | tf_op jit(solution)/shard_map/reduce_scatter | solution.py:143
  146.5 29.3 %all-gather.10.cloned.1.call-done = bf16[1024,1024]{1,0:T(8,128)(2,1)} async-done(((bf16[512,1024]{1,0:T(8,128)(2,1)}), bf16[1024,1024]{1,0:T(8,128)(2,1)}) %all-gather.10.cloned.1.call-update) | async-done | bytes 2097168 | tf_op jit(solution)/shard_map/all_gather | solution.py:183
  181.9 29.1 %all-gather.12.cloned.1.call-done = bf16[1024,1024]{1,0:T(8,128)(2,1)} async-done(((bf16[512,1024]{1,0:T(8,128)(2,1)}), bf16[1024,1024]{1,0:T(8,128)(2,1)}) %all-gather.12.cloned.1.call-update) | async-done | bytes 2097168 | tf_op jit(solution)/shard_map/all_gather | solution.py:147
  225.2 13.8 fusion.3
  258.2 54.4 %reduce-scatter.14.cloned.1.call-done = f32[512,1024]{1,0:T(8,128)} async-done(((f32[1024,1024]{1,0:T(8,128)}), f32[512,1024]{1,0:T(8,128)}) %reduce-scatter.14.cloned.1.call-update) | async-done | bytes 2097168 | tf_op jit(solution)/shard_map/reduce_scatter | solution.py:143
  318.0 32.5 %all-gather.14.cloned.1.call-done = bf16[1024,1024]{1,0:T(8,128)(2,1)} async-done(((bf16[512,1024]{1,0:T(8,128)(2,1)}), bf16[1024,1024]{1,0:T(8,128)(2,1)}) %all-gather.14.cloned.1.call-update) | async-done | bytes 2097168 | tf_op jit(solution)/shard_map/all_gather | solution.py:147
  350.5 25.9 %fusion.10 = (bf16[1024,2048]{1,0:T(8,128)(2,1)}, f32[1024,2048]{1,0:T(8,128)}) fusion(f32[2048]{0:T(1024)S(1)} %copy-done.93, bf16[1024,1024]{1,0:T(8,128)(2,1)} %all-gather.14.cloned.1.call-done, bf16[2048,1024]{1,0:T(8,128)(2,1)} %param.20), kind=kOutput, calls=%fused_computation.37 | convolution fusion | flops 4433379328 | bytes 18882560 | tf_op jit(solution)/shard_map/dot_general | solution.py:41
  385.2 11.5 convert_reduce_fusion
  415.1 44.0 %reduce-scatter.18.cloned.1.call-done = f32[512,1024]{1,0:T(8,128)} async-done(((f32[1024,1024]{1,0:T(8,128)}), f32[512,1024]{1,0:T(8,128)}) %reduce-scatter.18.cloned.1.call-update) | async-done | bytes 2097168 | tf_op jit(solution)/shard_map/reduce_scatter | solution.py:155
  462.2 53.7 %reduce-scatter.16.cloned.1.call-done = f32[512,1024]{1,0:T(8,128)} async-done(((f32[1024,1024]{1,0:T(8,128)}), f32[512,1024]{1,0:T(8,128)}) %reduce-scatter.16.cloned.1.call-update) | async-done | bytes 2097168 | tf_op jit(solution)/shard_map/reduce_scatter | solution.py:143
  523.0 33.2 %all-gather.18.cloned.1.call-done = bf16[1024,1024]{1,0:T(8,128)(2,1)} async-done(((bf16[512,1024]{1,0:T(8,128)(2,1)}), bf16[1024,1024]{1,0:T(8,128)(2,1)}) %all-gather.18.cloned.1.call-update) | async-done | bytes 2097168 | tf_op jit(solution)/shard_map/all_gather | solution.py:151
  559.9 15.5 %multiply_reduce_fusion.3 = (f32[8,512]{1,0:T(8,128)S(1)}, f32[8,512,1024]{2,1,0:T(8,128)}) fusion(f32[8,512,1024]{2,1,0:T(8,128)} %copy-done.2, f32[8,512]{1,0:T(8,128)S(1)} %log_add_fusion.3, bf16[512,8,64]{0,2,1:T(8,128)(2,1)S(1)} %bitcast.253, bf16[1024,8,64]{0,2,1:T(8,128)(2,1)S(1)} %copy-done.22), kind=kOutput, calls=%fused_computation.10 | convolution fusion | flops 549449728 | bytes 35160064 | tf_op jit(solution)/shard_map/qhe,khe->hqk/dot_general | solution.py:118
  593.7 14.5 %multiply_reduce_fusion.2 = (f32[8,512]{1,0:T(8,128)S(1)}, f32[8,512,1024]{2,1,0:T(8,128)}) fusion(f32[8,512,1024]{2,1,0:T(8,128)} %get-tuple-element.81, f32[8,512]{1,0:T(8,128)S(1)} %log_add_fusion.2, bf16[512,8,64]{0,2,1:T(8,128)(2,1)} %bitcast.255, bf16[1024,8,64]{0,2,1:T(8,128)(2,1)S(1)} %copy-done.22), kind=kOutput, calls=%fused_computation.7 | convolution fusion | flops 549449728 | bytes 35160064 | tf_op jit(solution)/shard_map/qhe,khe->hqk/dot_general | solution.py:118
  632.0 54.2 %reduce-scatter.20.cloned.1.call-done = f32[512,1024]{1,0:T(8,128)} async-done(((f32[1024,1024]{1,0:T(8,128)}), f32[512,1024]{1,0:T(8,128)}) %reduce-scatter.20.cloned.1.call-update) | async-done | bytes 2097168 | tf_op jit(solution)/shard_map/reduce_scatter | solution.py:241
  696.7 29.9 %all-gather.20.cloned.1.call-done = bf16[1024,1024]{1,0:T(8,128)(2,1)} async-done(((bf16[512,1024]{1,0:T(8,128)(2,1)}), bf16[1024,1024]{1,0:T(8,128)(2,1)}) %all-gather.20.cloned.1.call-update) | async-done | bytes 2097168 | tf_op jit(solution)/shard_map/all_gather | solution.py:151
  749.1 14.1 multiply_reduce_fusion.1
  771.6 11.9 multiply_convert_fusion.1
  870.7 12.7 copy.37
  928.3 90.1 %reduce-scatter.26.cloned.1.call-done = f32[3072,64]{0,1:T(8,128)} async-done(((f32[3072,1024]{0,1:T(8,128)}), f32[3072,64]{0,1:T(8,128)}) %reduce-scatter.26.cloned.1.call-update) | async-done | bytes 786448 | tf_op jit(solution)/shard_map/reduce_scatter | solution.py:268
  1021.4 106.7 %reduce-scatter.30.cloned.1.call-done = f32[2048,64]{0,1:T(8,128)} async-done(((f32[2048,1024]{0,1:T(8,128)}), f32[2048,64]{0,1:T(8,128)}) %reduce-scatter.30.cloned.1.call-update) | async-done | bytes 524304 | tf_op jit(solution)/shard_map/reduce_scatter | solution.py:280
  1128.2 109.4 %reduce-scatter.32.cloned.1.call-done = f32[2048,64]{0,1:T(8,128)} async-done(((f32[2048,1024]{0,1:T(8,128)}), f32[2048,64]{0,1:T(8,128)}) %reduce-scatter.32.cloned.1.call-update) | async-done | bytes 524304 | tf_op jit(solution)/shard_map/reduce_scatter | solution.py:281
  1237.6 56.7 %reduce-scatter.24.cloned.1.call-done = f32[512,1024]{1,0:T(8,128)} async-done(((f32[1024,1024]{1,0:T(8,128)}), f32[512,1024]{1,0:T(8,128)}) %reduce-scatter.24.cloned.1.call-update) | async-done | bytes 2097168 | tf_op jit(solution)/shard_map/reduce_scatter | solution.py:244
  1294.3 132.6 %all-reduce.3.cloned.1.call-done = (f32[2,2,1024]{2,1,0:T(2,128)}, f32[4096]{0:T(1024)}, f32[3,1024]{1,0:T(4,128)}, f32[3,1024]{1,0:T(4,128)}, f32[3,1024]{1,0:T(4,128)}) async-done(((f32[2,2,1024]{2,1,0:T(2,128)}, f32[4096]{0:T(1024)}, f32[3,1024]{1,0:T(4,128)}, f32[3,1024]{1,0:T(4,128)}, f32[3,1024]{1,0:T(4,128)}), (f32[2,2,1024]{2,1,0:T(2,128)}, f32[4096]{0:T(1024)}, f32[3,1024]{1,0:T(4,128)}, ...) | async-done | bytes 69648 | tf_op jit(solution)/shard_map/psum | solution.py:308
  (417 shorter events, 363.4 us)
Async XLA Ops:
  7.2 42.0 %all-gather.8.cloned.1.call-start = ((), (), s32[]{:S(2)}) async-start(), calls=%async_computation.11 | async-start | bytes 3145728 | tf_op jit(solution)/shard_map/all_gather | solution.py:182
  11.2 132.2 %copy-start.57 = (f32[1,1024]{1,0:T(1,128)}, f32[1,1024]{1,0:T(1,128)S(1)}, u32[]{:S(2)}) copy-start(f32[1,1024]{1,0:T(1,128)S(1)} %get-tuple-element.66) | copy-start | bytes 12292
  14.7 126.3 %reduce-scatter.12.cloned.1.call-start = ((), (), s32[]{:S(2)}) async-start(), calls=%async_computation.12 | async-start | bytes 6291456 | tf_op jit(solution)/shard_map/reduce_scatter | solution.py:143
  86.6 89.2 %all-gather.10.cloned.1.call-start = ((), (), s32[]{:S(2)}) async-start(), calls=%async_computation.13 | async-start | bytes 3145728 | tf_op jit(solution)/shard_map/all_gather | solution.py:183
  87.3 123.7 %all-gather.12.cloned.1.call-start = ((), (), s32[]{:S(2)}) async-start(), calls=%async_computation.14 | async-start | bytes 3145728 | tf_op jit(solution)/shard_map/all_gather | solution.py:147
  143.0 169.6 %copy-start.6 = (f32[512,1024]{1,0:T(8,128)}, f32[512,1024]{1,0:T(8,128)S(1)}, u32[]{:S(2)}) copy-start(f32[512,1024]{1,0:T(8,128)S(1)} %get-tuple-element.50) | copy-start | bytes 6291460
  144.8 167.7 %reduce-scatter.14.cloned.1.call-start = ((), (), s32[]{:S(2)}) async-start(), calls=%async_computation.15 | async-start | bytes 6291456 | tf_op jit(solution)/shard_map/reduce_scatter | solution.py:143
  258.1 92.4 %all-gather.14.cloned.1.call-start = ((), (), s32[]{:S(2)}) async-start(), calls=%async_computation.16 | async-start | bytes 3145728 | tf_op jit(solution)/shard_map/all_gather | solution.py:147
  317.2 68.0 %all-gather.16.cloned.1.call-start = ((), (), s32[]{:S(2)}) async-start(), calls=%async_computation.18 | async-start | bytes 3145728 | tf_op jit(solution)/shard_map/all_gather | solution.py:151
  317.9 141.2 %reduce-scatter.18.cloned.1.call-start = ((), (), s32[]{:S(2)}) async-start(), calls=%async_computation.19 | async-start | bytes 6291456 | tf_op jit(solution)/shard_map/reduce_scatter | solution.py:155
  404.7 111.2 %reduce-scatter.16.cloned.1.call-start = ((), (), s32[]{:S(2)}) async-start(), calls=%async_computation.17 | async-start | bytes 6291456 | tf_op jit(solution)/shard_map/reduce_scatter | solution.py:143
  415.1 100.8 %copy-start.80 = (f32[1,1024]{1,0:T(1,128)S(1)}, f32[1,1024]{1,0:T(1,128)}, u32[]{:S(2)}) copy-start(f32[1,1024]{1,0:T(1,128)} %get-tuple-element.61) | copy-start | bytes 12292
  415.1 141.1 %all-gather.18.cloned.1.call-start = ((), (), s32[]{:S(2)}) async-start(), calls=%async_computation.20 | async-start | bytes 3145728 | tf_op jit(solution)/shard_map/all_gather | solution.py:151
  522.9 163.4 %reduce-scatter.20.cloned.1.call-start = ((), (), s32[]{:S(2)}) async-start(), calls=%async_computation.21 | async-start | bytes 6291456 | tf_op jit(solution)/shard_map/reduce_scatter | solution.py:241
  631.8 54.5 %copy-start.66 = (f32[512]{0:T(512)S(1)}, f32[512]{0:T(512)}, u32[]{:S(2)}) copy-start(f32[512]{0:T(512)} %copy-done.65) | copy-start | bytes 6148
  631.8 54.5 %copy-start.70 = (f32[512]{0:T(512)S(1)}, f32[512]{0:T(512)}, u32[]{:S(2)}) copy-start(f32[512]{0:T(512)} %copy-done.69) | copy-start | bytes 6148
  631.8 94.8 %all-gather.20.cloned.1.call-start = ((), (), s32[]{:S(2)}) async-start(), calls=%async_computation.22 | async-start | bytes 3145728 | tf_op jit(solution)/shard_map/all_gather | solution.py:151
  693.3 225.7 %reduce-scatter.28.cloned.1.call-start = ((), (), s32[]{:S(2)}) async-start(), calls=%async_computation.26 | async-start | bytes 4456448 | tf_op jit(solution)/shard_map/reduce_scatter | solution.py:274
  740.3 180.6 %reduce-scatter.22.cloned.1.call-start = ((), (), s32[]{:S(2)}) async-start(), calls=%async_computation.23 | async-start | bytes 6291456 | tf_op jit(solution)/shard_map/reduce_scatter | solution.py:155
  825.4 193.0 %reduce-scatter.26.cloned.1.call-start = ((), (), s32[]{:S(2)}) async-start(), calls=%async_computation.25 | async-start | bytes 13369344 | tf_op jit(solution)/shard_map/reduce_scatter | solution.py:268
  883.3 244.8 %reduce-scatter.30.cloned.1.call-start = ((), (), s32[]{:S(2)}) async-start(), calls=%async_computation.27 | async-start | bytes 8912896 | tf_op jit(solution)/shard_map/reduce_scatter | solution.py:280
  894.2 343.3 %reduce-scatter.32.cloned.1.call-start = ((), (), s32[]{:S(2)}) async-start(), calls=%async_computation.28 | async-start | bytes 8912896 | tf_op jit(solution)/shard_map/reduce_scatter | solution.py:281
  905.8 388.4 %reduce-scatter.24.cloned.1.call-start = ((), (), s32[]{:S(2)}) async-start(), calls=%async_computation.24 | async-start | bytes 6291456 | tf_op jit(solution)/shard_map/reduce_scatter | solution.py:244
  914.5 512.4 %all-reduce.3.cloned.1.call-start = ((), (), s32[]{:S(2)}) async-start(), calls=%async_computation.29 | async-start | bytes 163840 | tf_op jit(solution)/shard_map/psum | solution.py:308
  (114 other events, 1261.8 us)
Sparse Core Ops, SparseCore 0:
  14.9 34.2 all-gather.7
  86.7 54.2 reduce-scatter.11
  142.7 33.1 all-gather.9
  177.9 33.1 all-gather.11
  258.2 54.2 reduce-scatter.13
  317.3 33.1 all-gather.13
  352.0 33.1 all-gather.15
  404.8 54.2 reduce-scatter.17
  461.5 54.3 reduce-scatter.15
  523.0 33.1 all-gather.17
  631.9 54.2 reduce-scatter.19
  693.4 33.1 all-gather.19
  740.4 71.7 reduce-scatter.27
  825.5 54.3 reduce-scatter.21
  884.3 134.0 reduce-scatter.25
  1023.4 104.6 reduce-scatter.29
  1133.2 104.3 reduce-scatter.31
  1240.4 53.8 reduce-scatter.23
  1301.8 125.0 all-reduce.2
where the time goes:
time: 1450 us; the launch traced here: 1440 us
  waiting for transfers between devices  951 us (66%)
  matrix products  282 us (19%)
  other arithmetic  121 us (8%)
  local copies, waits for them, and re-layouts  68.8 us (5%)
  between operations  16.3 us (1%)
    reduce_scatter x3, waiting for transfers between devices, branch_total(): lax.psum_scatter(branch_part, 'tensor', scatter_dimension=0, tiled=True)  161 us
    psum x1, waiting for transfers between devices, shards(): lax.psum((bias_full, up_bias_full, out_bias_terms, gain_terms, shift_term...  133 us
    reduce_scatter x1, waiting for transfers between devices, shards(): lax.psum_scatter(grad_down, 'dp', scatter_dimension=1, tiled=True)  109 us
    reduce_scatter x1, waiting for transfers between devices, shards(): lax.psum_scatter(grad_up, 'dp', scatter_dimension=1, tiled=True)  107 us
    reduce_scatter x1, waiting for transfers between devices, shards(): lax.psum_scatter(jnp.stack([grad_in_one, grad_in_two]).reshape(-1, D), 'd...  90.1 us
    all_gather x3, waiting for transfers between devices, gather_grads(): return lax.all_gather(gradient, 'tensor', axis=0, tiled=True)  71.9 us
    all_gather x2, waiting for transfers between devices, gather_normed(): return lax.all_gather(normed, 'tensor', axis=0, tiled=True)  61.6 us
    reduce_scatter x1, waiting for transfers between devices, shards(): lax.psum_scatter(memory_part, 'tensor', scatter_dimension=0, tiled=True)  56.7 us
  transfers between devices with their start and end apart: 19, of which 17 were waited for; matrix products, arithmetic and copies ran while one was open for 16% of the time, Pallas kernels for 0%

commit v1 on v0

v1 whole, which is shorter than its diff:
```python
import functools

import jax
import jax.numpy as jnp
from jax import lax
from jax.experimental import pallas as pl
from jax.experimental.pallas import tpu as pltpu
from jax.sharding import PartitionSpec as P

HEAD_DIM = 64
F32 = jnp.float32
BF = jnp.bfloat16
NT = (((1,), (1,)), ((), ()))
TN = (((0,), (0,)), ((), ()))
NN = (((1,), (0,)), ((), ()))

epsilon = 1e-05
masked_score = -1e30
root_half = 0.7071067811865476
normal_peak = 0.3989422804014327
score_scale = HEAD_DIM ** (-0.5)


def mm(left, right, dims=NN):
    return lax.dot_general(left, right, dims, preferred_element_type=F32)


def three_parts(values):
    top = values.astype(BF).astype(F32)
    rest = values - top
    middle = rest.astype(BF).astype(F32)
    return top, middle, rest - middle


def attend_kernel(causal, step, len_ref, q_ref, k_ref, v_ref, o_ref, sum_ref):
    length = len_ref[0]
    rows, keys = q_ref.shape[0], k_ref.shape[0]
    lane = lax.broadcasted_iota(jnp.int32, (1, 128), 1)
    key_pos = lax.broadcasted_iota(jnp.int32, (keys, 1), 0)
    bias = jnp.where(key_pos < length, 0.0, masked_score)
    q = q_ref[...].astype(F32) * score_scale
    k = k_ref[...].astype(F32)
    v = v_ref[...].astype(F32)
    sides = []
    for head in range(2):
        own = (lane < 64) if head == 0 else (lane >= 64)
        first = lane == (64 if head == 0 else 0)
        q_wide = jnp.where(own, q, jnp.where(first, 1.0, 0.0)).astype(BF)
        k_wide = jnp.where(own, k, jnp.where(first, bias, 0.0)).astype(BF)
        v_wide = jnp.where(own, v, 1.0).astype(BF)
        sides.append((q_wide, k_wide, v_wide))
    for block in range(rows // step):
        here = slice(block * step, (block + 1) * step)
        reach = (block + 1) * step if causal else keys
        parts = []
        for head in range(2):
            q_wide, k_wide, v_wide = sides[head]
            scores = mm(q_wide[here], k_wide[:reach], NT)
            if causal:
                below = lax.broadcasted_iota(jnp.int32, (step, step), 1) <= lax.broadcasted_iota(
                    jnp.int32, (step, step), 0
                )
                edge = jnp.where(below, scores[:, reach - step :], masked_score)
                if block == 0:
                    scores = edge
                else:
                    scores = jnp.concatenate([scores[:, : reach - step], edge], axis=1)
            top = jnp.max(scores, axis=1, keepdims=True)
            weights = jnp.exp(scores - top).astype(BF)
            mixed = mm(weights, v_wide[:reach])
            total = mixed[:, 64:65] if head == 0 else mixed[:, 0:1]
            parts.append((mixed / total, top + jnp.log(total)))
        o_ref[here, :] = jnp.where(lane < 64, parts[0][0], parts[1][0]).astype(BF)
        sum_ref[here, :] = jnp.where(lane < 64, parts[0][1], parts[1][1])


def attend_back_kernel(
    causal, step, len_ref, q_ref, k_ref, v_ref, g_ref, o_ref, sum_ref,
    dq_ref, dk_ref, dv_ref, acc_ref,
):
    length = len_ref[0]
    rows, keys = q_ref.shape[0], k_ref.shape[0]
    lane = lax.broadcasted_iota(jnp.int32, (1, 128), 1)
    key_pos = lax.broadcasted_iota(jnp.int32, (keys, 1), 0)
    bias = jnp.where(key_pos < length, 0.0, masked_score)
    q = q_ref[...].astype(F32) * score_scale
    k = k_ref[...].astype(F32)
    v = v_ref[...].astype(F32)
    g = g_ref[...].astype(F32)
    overlap = g * o_ref[...].astype(F32)
    log_sums = sum_ref[...]
    sides = []
    for head in range(2):
        own = (lane < 64) if head == 0 else (lane >= 64)
        base = 64 if head == 0 else 0
        at = [lane == base + i for i in range(4)]
        minus = jnp.where(at[1] | at[2] | at[3], -1.0, 0.0)
        delta = jnp.sum(jnp.where(own, overlap, 0.0), axis=1, keepdims=True)
        log_sum = log_sums[:, 0:1] if head == 0 else log_sums[:, 64:65]
        s0, s1, s2 = three_parts(log_sum)
        d0, d1, d2 = three_parts(delta)
        extra_q = jnp.where(
            at[0], 1.0, jnp.where(at[1], s0, jnp.where(at[2], s1, jnp.where(at[3], s2, 0.0)))
        )
        extra_g = jnp.where(at[1], d0, jnp.where(at[2], d1, jnp.where(at[3], d2, 0.0)))
        q_wide = jnp.where(own, q, extra_q).astype(BF)
        k_wide = jnp.where(own, k, jnp.where(at[0], bias, minus)).astype(BF)
        g_wide = jnp.where(own, g, extra_g).astype(BF)
        v_wide = jnp.where(own, v, minus).astype(BF)
        sides.append((q_wide, k_wide, g_wide, v_wide))
    for block in range(keys // step):
        here = slice(block * step, (block + 1) * step)
        low = block * step if causal else 0
        dks = []
        dvs = []
        for head in range(2):
            q_wide, k_wide, g_wide, v_wide = sides[head]
            scores = mm(k_wide[here], q_wide[low:], NT)
            if causal:
                below = lax.broadcasted_iota(jnp.int32, (step, step), 0) <= lax.broadcasted_iota(
                    jnp.int32, (step, step), 1
                )
                edge = jnp.where(below, scores[:, :step], masked_score)
                if low + step == rows:
                    scores = edge
                else:
                    scores = jnp.concatenate([edge, scores[:, step:]], axis=1)
            probs = jnp.exp(scores)
            grads = (probs * mm(v_wide[here], g_wide[low:], NT)).astype(BF)
            dvs.append(mm(probs.astype(BF), g_wide[low:]))
            dks.append(mm(grads, q_wide[low:]))
            dq = mm(grads, k_wide[here], TN)
            if block == 0:
                acc_ref[head] = dq
            else:
                acc_ref[head, low:, :] += dq
        dv_ref[here, :] = jnp.where(lane < 64, dvs[0], dvs[1]).astype(BF)
        dk_ref[here, :] = jnp.where(lane < 64, dks[0], dks[1]).astype(BF)
    dq_ref[...] = (jnp.where(lane < 64, acc_ref[0], acc_ref[1]) * score_scale).astype(BF)


def pair_spec(rows):
    return pl.BlockSpec((rows, 128), lambda i: (0, i))


def attend(q, k, v, length, causal):
    rows, width = q.shape
    keys = k.shape[0]
    return pl.pallas_call(
        functools.partial(attend_kernel, causal, 256),
        grid=(width // 128,),
        in_specs=[
            pl.BlockSpec(memory_space=pltpu.SMEM),
            pair_spec(rows),
            pair_spec(keys),
            pair_spec(keys),
        ],
        out_specs=[pair_spec(rows), pair_spec(rows)],
        out_shape=[
            jax.ShapeDtypeStruct((rows, width), BF),
            jax.ShapeDtypeStruct((rows, width), F32),
        ],
        compiler_params=pltpu.CompilerParams(vmem_limit_bytes=40 << 20),
        cost_estimate=pl.CostEstimate(
            flops=16 * rows * keys * width,
            bytes_accessed=8 * rows * width,
            transcendentals=rows * keys * width // 64,
        ),
    )(length, q, k, v)


def attend_back(q, k, v, grad, out, sums, length, causal):
    rows, width = q.shape
    keys = k.shape[0]
    return pl.pallas_call(
        functools.partial(attend_back_kernel, causal, 256),
        grid=(width // 128,),
        in_specs=[
            pl.BlockSpec(memory_space=pltpu.SMEM),
            pair_spec(rows),
            pair_spec(keys),
            pair_spec(keys),
            pair_spec(rows),
            pair_spec(rows),
            pair_spec(rows),
        ],
        out_specs=[pair_spec(rows), pair_spec(keys), pair_spec(keys)],
        out_shape=[
            jax.ShapeDtypeStruct((rows, width), BF),
            jax.ShapeDtypeStruct((keys, width), BF),
            jax.ShapeDtypeStruct((keys, width), BF),
        ],
        scratch_shapes=[pltpu.VMEM((2, rows, 128), F32)],
        compiler_params=pltpu.CompilerParams(vmem_limit_bytes=40 << 20),
        cost_estimate=pl.CostEstimate(
            flops=40 * rows * keys * width,
            bytes_accessed=16 * rows * width,
            transcendentals=rows * keys * width // 64,
        ),
    )(length, q, k, v, grad, out, sums)


def normalize(values, gain_row, shift_row):
    centred = values - jnp.mean(values, axis=-1, keepdims=True)
    inverse = lax.rsqrt(jnp.mean(centred * centred, axis=-1, keepdims=True) + epsilon)
    unit_rows = centred * inverse
    return ((unit_rows * gain_row + shift_row).astype(BF), unit_rows, inverse)


def normalize_back(gradient, unit_rows, inverse, gain_row):
    scaled = gradient * gain_row
    return inverse * (
        scaled
        - jnp.mean(scaled, axis=-1, keepdims=True)
        - unit_rows * jnp.mean(scaled * unit_rows, axis=-1, keepdims=True)
    )


def gelu_parts(values):
    below = 0.5 * (1.0 + lax.erf(values * root_half))
    slope = below + values * jnp.exp(-0.5 * values * values) * normal_peak
    return (values * below).astype(BF), slope


def take(array, index, axis=0):
    return lax.dynamic_index_in_dim(array, index, axis, keepdims=False)


def make_shards(mesh):
    dp_size = mesh.shape["dp"]
    bits = dp_size.bit_length() - 1

    def shards(
        hidden_in, memory, in_proj, in_bias, out_proj, ffn_up, ffn_up_bias, ffn_down, out_bias,
        norm_gain, norm_bias, out_grad, target_len, source_len, assignment,
    ):
        dp = lax.axis_index("dp")
        side = lax.axis_index("tensor")
        core = dp & 1
        bit = [(dp >> i) & 1 for i in range(bits)]

        def over(array, i):
            return lax.ppermute(array, "dp", [(d, d ^ (1 << i)) for d in range(dp_size)])

        def across(array):
            return lax.ppermute(array, "tensor", [(0, 1), (1, 0)])

        def slot_swap(array):
            pairs = []
            for j in range(dp_size // 2):
                pairs += [(4 * j + 1, 4 * j + 2), (4 * j + 2, 4 * j + 1)]
            got = lax.ppermute(array, ("dp", "tensor"), pairs)
            return got

        def to_row(array):
            got = slot_swap(array)
            return jnp.where(core == side, array, got)

        def from_row(array):
            got = slot_swap(array.astype(BF))
            return jnp.where(core == side, array, got.astype(array.dtype))

        def whole_row(half):
            other = over(half, 0)
            return jnp.concatenate(
                [jnp.where(core == 0, half, other), jnp.where(core == 0, other, half)], axis=0
            )

        def core_sum(part):
            return part + over(part.astype(BF), 0).astype(F32)

        def half_of(array, index):
            return take(array.reshape(2, array.shape[0] // 2, -1), index)

        def core_scatter(part):
            other = over(half_of(part, 1 - core).astype(BF), 0)
            return half_of(part, core) + other.astype(F32)

        own_row = jnp.broadcast_to(assignment.reshape(1, 1).astype(F32), (8, 128))
        held = jnp.where(core == side, own_row, over(own_row, 0))[0, 0].astype(jnp.int32)
        row_ids = lax.iota(jnp.int32, target_len.shape[0])
        target_length = jnp.sum(jnp.where(row_ids == held, target_len, 0)).reshape(1)
        source_length = jnp.sum(jnp.where(row_ids == held, source_len, 0)).reshape(1)

        hidden_half = to_row(hidden_in)
        hidden_row = whole_row(hidden_half)

        def quarter(array, axis):
            shape = array.shape
            split = shape[:axis] + (2, shape[axis] // 2) + shape[axis + 1 :]
            return take(array.reshape(split), core, axis)

        def fetch(part, axis):
            shape = part.shape
            split = shape[:axis] + (4, shape[axis] // 4) + shape[axis + 1 :]
            pieces = part.reshape(split)
            place = bit[1] + 2 * bit[2]
            first = across(take(pieces, place, axis))
            by_y = over(first, 1)
            by_z = over(first, 2)
            cut = first.shape[-1] // 2
            last = jnp.concatenate(
                [over(by_y[..., :cut], 2), over(by_z[..., cut:], 1)], axis=-1
            )
            out = jnp.zeros(split, part.dtype)
            for piece, spot in ((first, place), (by_y, place ^ 1), (by_z, place ^ 2), (last, place ^ 3)):
                out = lax.dynamic_update_slice_in_dim(out, jnp.expand_dims(piece, axis), spot, axis)
            return out.reshape(shape)

        def both(part, axis):
            return jnp.concatenate([part, fetch(part, axis)], axis=axis)

        bias_part = jnp.concatenate(
            [quarter(in_bias, 2).reshape(-1), quarter(ffn_up_bias, 0)], axis=0
        )
        far_bias = across(bias_part)
        head_part = in_bias.shape[2] // 2
        in_bias_own = jnp.concatenate(
            [
                bias_part[: 4 * head_part].reshape(2, 2, head_part),
                far_bias[: 4 * head_part].reshape(2, 2, head_part),
            ],
            axis=2,
        )
        up_bias_own = jnp.concatenate([bias_part[4 * head_part :], far_bias[4 * head_part :]])

        in_quarter = quarter(in_proj, 2)
        w_self = both(in_quarter[0], 1)
        memory_row = whole_row(to_row(memory))
        w_cross = both(in_quarter[1], 1)
        w_out = both(quarter(out_proj, 1), 1)
        w_up = both(quarter(ffn_up, 0), 0)
        w_down = both(quarter(ffn_down, 0), 0)
        grad_half = to_row(out_grad)
        grad_row = whole_row(grad_half)

        stream_zero = hidden_row.astype(F32)
        rows_one, unit_one, inverse_one = normalize(stream_zero, norm_gain[0], norm_bias[0])
        query_one = (mm(rows_one, w_self[0], NT) + in_bias_own[0, 0]).astype(BF)
        key_one = mm(rows_one, w_self[1], NT).astype(BF)
        value_one = (mm(rows_one, w_self[2], NT) + in_bias_own[0, 1]).astype(BF)
        mixed_one, sums_one = attend(query_one, key_one, value_one, target_length, True)
        stream_one = stream_zero + core_sum(mm(mixed_one, w_out[0])) + out_bias[0]

        rows_two, unit_two, inverse_two = normalize(stream_one, norm_gain[1], norm_bias[1])
        key_two = mm(memory_row, w_cross[1], NT).astype(BF)
        value_two = (mm(memory_row, w_cross[2], NT) + in_bias_own[1, 1]).astype(BF)
        query_two = (mm(rows_two, w_cross[0], NT) + in_bias_own[1, 0]).astype(BF)
        mixed_two, sums_two = attend(query_two, key_two, value_two, source_length, False)
        stream_two = stream_one + core_sum(mm(mixed_two, w_out[1])) + out_bias[1]

        rows_three, unit_three, inverse_three = normalize(stream_two, norm_gain[2], norm_bias[2])
        active, slope = gelu_parts(mm(rows_three, w_up, NT) + up_bias_own)
        hidden_out = from_row(
            (half_of(stream_two, core) + core_scatter(mm(active, w_down)) + out_bias[2]).astype(BF)
        )

        def reduce_grad(rows_mat, cols_mat):
            count, kinds, _, width = cols_mat.shape
            there = cols_mat[:, :, 1].reshape(count, kinds * width)
            here = cols_mat[:, :, 0].reshape(count, kinds * width)
            arrived = across(mm(rows_mat, there, TN).astype(BF))
            kept = mm(rows_mat, here, TN) + arrived.astype(F32)
            kept = kept.reshape((2,) * bits + (-1, kinds * width))
            done = []
            for i in range(1, bits):
                axis = bits - 1 - i - sum(1 for j in done if j > i)
                arrived = over(take(kept, 1 - bit[i], axis).astype(BF), i)
                kept = take(kept, bit[i], axis) + arrived.astype(F32)
                done.append(i)
            arrived = over(take(kept, 1 - core), 0)
            kept = take(kept, core)
            first = jnp.where(core == 0, kept, arrived).reshape(-1, kinds, width)
            second = jnp.where(core == 0, arrived, kept).reshape(-1, kinds, width)
            total = jnp.concatenate([first, second], axis=2)
            return jnp.transpose(total, (1, 2, 0))

        def parted(array):
            return array.reshape(array.shape[0], 1, 2, -1)

        down_share = reduce_grad(grad_row, parted(active))[0]
        grad_active = mm(grad_row, w_down, NT).astype(BF)
        grad_pre = (grad_active.astype(F32) * slope).astype(BF)
        up_share = reduce_grad(rows_three, parted(grad_pre))[0]
        back_three = core_sum(mm(grad_pre, w_up))
        grad_two = grad_row.astype(F32) + normalize_back(
            back_three, unit_three, inverse_three, norm_gain[2]
        )

        down_two = grad_two.astype(BF)
        out_share_two = reduce_grad(down_two, parted(mixed_two))
        grad_mixed_two = mm(down_two, w_out[1], NT).astype(BF)
        dq_two, dk_two, dv_two = attend_back(
            query_two, key_two, value_two, grad_mixed_two, mixed_two, sums_two, source_length, False
        )
        q_share_two = reduce_grad(rows_two, parted(dq_two))
        kv_share_two = reduce_grad(memory_row, jnp.stack([dk_two, dv_two], axis=1).reshape(dk_two.shape[0], 2, 2, -1))
        memory_grad = from_row(core_scatter(mm(dk_two, w_cross[1]) + mm(dv_two, w_cross[2])))
        back_two = core_sum(mm(dq_two, w_cross[0]))
        grad_one = grad_two + normalize_back(back_two, unit_two, inverse_two, norm_gain[1])

        down_one = grad_one.astype(BF)
        out_share_one = reduce_grad(down_one, parted(mixed_one))
        grad_mixed_one = mm(down_one, w_out[0], NT).astype(BF)
        dq_one, dk_one, dv_one = attend_back(
            query_one, key_one, value_one, grad_mixed_one, mixed_one, sums_one, target_length, True
        )
        in_share_one = reduce_grad(
            rows_one, jnp.stack([dq_one, dk_one, dv_one], axis=1).reshape(dq_one.shape[0], 3, 2, -1)
        )
        back_one = core_scatter(
            mm(dq_one, w_self[0]) + mm(dk_one, w_self[1]) + mm(dv_one, w_self[2])
        )
        unit_one_half = half_of(unit_one, core)
        grad_one_half = half_of(grad_one, core)
        hidden_grad = from_row(
            grad_one_half
            + normalize_back(back_one, unit_one_half, half_of(inverse_one, core), norm_gain[0])
        )

        in_proj_grad = jnp.stack([in_share_one, jnp.concatenate([q_share_two, kv_share_two])])
        out_proj_grad = jnp.concatenate([out_share_one, out_share_two])

        def placed(array, size):
            width = array.shape[-1] // 2
            out = jnp.zeros(array.shape[:-1] + (size // width, width), F32)
            axis = out.ndim - 2
            for part, half in ((array[..., :width], side), (array[..., width:], 1 - side)):
                out = lax.dynamic_update_slice_in_dim(
                    out, jnp.expand_dims(part, axis), half * 2 + core, axis
                )
            return out.reshape(array.shape[:-1] + (size,))

        def col_sum(array):
            return jnp.sum(array.astype(F32), axis=0)

        in_bias_part = placed(
            jnp.stack(
                [
                    jnp.stack([col_sum(dq_one), col_sum(dv_one)]),
                    jnp.stack([col_sum(dq_two), col_sum(dv_two)]),
                ]
            ),
            4 * head_part,
        )
        up_bias_part = placed(col_sum(grad_pre), 2 * ffn_up_bias.shape[0])
        back_three_half = half_of(back_three, core)
        back_two_half = half_of(back_two, core)
        model_part = jnp.stack(
            [
                col_sum(grad_one_half),
                col_sum(half_of(grad_two, core)),
                col_sum(grad_half),
                col_sum(back_one * unit_one_half),
                col_sum(back_two_half * half_of(unit_two, core)),
                col_sum(back_three_half * half_of(unit_three, core)),
                col_sum(back_one),
                col_sum(back_two_half),
                col_sum(back_three_half),
            ]
        )
        width = model_part.shape[1]
        sums = jnp.concatenate(
            [in_bias_part.reshape(-1, width), up_bias_part.reshape(-1, width), model_part]
        )
        for i in range(bits):
            sums = sums + over(sums, i)
        sums = sums + across(sums)
        in_bias_grad = sums[:4].reshape(2, 2, width)
        up_rows = up_bias_part.size // width
        ffn_up_bias_grad = sums[4 : 4 + up_rows].reshape(-1)
        out_bias_grad = sums[4 + up_rows : 7 + up_rows]
        norm_gain_grad = sums[7 + up_rows : 10 + up_rows]
        norm_bias_grad = sums[10 + up_rows : 13 + up_rows]
        return (
            hidden_out,
            hidden_grad,
            memory_grad,
            in_proj_grad,
            out_proj_grad,
            up_share,
            down_share,
            in_bias_grad,
            ffn_up_bias_grad,
            out_bias_grad,
            norm_gain_grad,
            norm_bias_grad,
        )

    return shards


def solution(mesh):
    return jax.shard_map(
        make_shards(mesh),
        mesh=mesh,
        in_specs=(
            P(("dp", "tensor"), None),
            P(("dp", "tensor"), None),
            P(None, None, "tensor", None),
            P(None, None, "tensor"),
            P(None, "tensor", None),
            P("tensor", None),
            P("tensor"),
            P("tensor", None),
            P(),
            P(),
            P(),
            P(("dp", "tensor"), None),
            P(),
            P(),
            P("dp"),
        ),
        out_specs=(
            P(("dp", "tensor"), None),
            P(("dp", "tensor"), None),
            P(("dp", "tensor"), None),
            P(None, None, "tensor", "dp"),
            P(None, "tensor", "dp"),
            P("tensor", "dp"),
            P("tensor", "dp"),
            P(),
            P(),
            P(),
            P(),
            P(),
        ),
        check_vma=False,
    )
```

time: 1450 us -> 785 us (0.54)
  waiting for transfers between devices: 951 us -> 223 us
  matrix products: 282 us -> 107 us
  starting transfers between devices: 1.61 us -> 159 us
  Pallas kernels: 0 us -> 81.2 us
  local copies, waits for them, and re-layouts: 68.8 us -> 124 us
  other arithmetic: 121 us -> 75.8 us
    reduce_scatter x11 -> x0, waiting for transfers between devices: 622 us -> none  [the longest x3 161 us: branch_total(): lax.psum_scatter(branch_part, 'tensor', scatter_dimension=0, tiled=True)]
    ppermute x0 -> x83, waiting for transfers between devices: none -> 223 us  [the longest x63 140 us: over(): return lax.ppermute(array, 'dp', [(d, d ^ 1 << i) for d in range(dp_size)])]
    all_gather x7 -> x0, waiting for transfers between devices: 195 us -> none  [the longest x3 71.9 us: gather_grads(): return lax.all_gather(gradient, 'tensor', axis=0, tiled=True)]
    dot_general x47 -> x34, matrix products: 282 us -> 107 us  [mm(): return lax.dot_general(left, right, dims, preferred_element_type=F32)]
    ppermute x0 -> x83, starting transfers between devices: none -> 159 us  [the longest x63 125 us: over(): return lax.ppermute(array, 'dp', [(d, d ^ 1 << i) for d in range(dp_size)])]
    psum x1 -> x0, waiting for transfers between devices: 133 us -> none  [shards(): lax.psum((bias_full, up_bias_full, out_bias_terms, gain_terms, shift_term...]
    pallas_call x0 -> x4, Pallas kernels: none -> 81.2 us  [the longest x2 48 us: attend_back(): pl.pallas_call(functools.partial(attend_back_kernel, causal, 256), grid=(...]
    convert_element_type x12 -> x7, other arithmetic: 49.6 us -> 15.5 us  [the longest x3 7.33 us: normalize(): return ((unit_rows * gain_row + shift_row).astype(BF), unit_rows, inverse)]
  transfers between devices with their start and end apart: 19 -> 83, of which waited for: 17 -> 32; matrix products, arithmetic and copies ran while one was open for 16% -> 28% of each run, Pallas kernels for 0% -> 10%
where the time goes in v1:
time: 785 us; the launch traced here: 775 us
  waiting for transfers between devices  223 us (28%)
  starting transfers between devices  159 us (20%)
  local copies, waits for them, and re-layouts  124 us (16%)
  matrix products  107 us (14%)
  Pallas kernels  81.2 us (10%)
  other arithmetic  75.8 us (10%)
    ppermute x63, waiting for transfers between devices, over(): return lax.ppermute(array, 'dp', [(d, d ^ 1 << i) for d in range(dp_size)])  140 us
    ppermute x63, starting transfers between devices, over(): return lax.ppermute(array, 'dp', [(d, d ^ 1 << i) for d in range(dp_size)])  125 us
    dot_general x34, matrix products, mm(): return lax.dot_general(left, right, dims, preferred_element_type=F32)  107 us
    ppermute x14, waiting for transfers between devices, across(): return lax.ppermute(array, 'tensor', [(0, 1), (1, 0)])  82.3 us
    pallas_call x2, Pallas kernels, attend_back(): pl.pallas_call(functools.partial(attend_back_kernel, causal, 256), grid=(...  48 us
    pallas_call x2, Pallas kernels, attend(): pl.pallas_call(functools.partial(attend_kernel, causal, 256), grid=(width...  33.2 us
    unnamed x247, local copies, waits for them, and re-layouts  30.1 us
    ppermute x14, starting transfers between devices, across(): return lax.ppermute(array, 'tensor', [(0, 1), (1, 0)])  26.5 us
  transfers between devices with their start and end apart: 83, of which 32 were waited for; matrix products, arithmetic and copies ran while one was open for 28% of the time, Pallas kernels for 10%

profile of v1, /device:TPU:8, one launch (start us, length us, event | category | flops | bytes accessed | tf_op | source)
XLA Modules:
  0.0 775.1 jit_solution(3514369020624322644)
XLA Ops:
  35.0 7.3 collective-permute-done.9
  51.7 7.5 collective-permute-done.11
  77.0 7.4 collective-permute-done.12
  103.6 14.9 %shard_map.238 = (bf16[1024,512]{1,0:T(8,128)(2,1)S(1)}, f32[1024,512]{1,0:T(8,128)S(1)}) custom-call(s32[1]{0:T(128)} %bitcast.2.len_ref, bf16[1024,512]{1,0:T(8,128)(2,1)S(1)} %add_convert_fusion.6.q_ref, bf16[1024,512]{1,0:T(8,128)(2,1)S(1)} %convolution_convert_fusion.5.k_ref, bf16[1024,512]{1,0:T(8,128)(2,1)S(1)} %add_convert_fusion.5.v_ref), custom_call_target="tpu_custom_call" | custom-call | flops 8589934592 | bytes 4194304 | tf_op jit(solution)/shard_map/pallas_call | solution.py:149
  126.0 7.4 collective-permute-done.24
  153.8 18.3 %shard_map.239 = (bf16[1024,512]{1,0:T(8,128)(2,1)S(1)}, f32[1024,512]{1,0:T(8,128)S(1)}) custom-call(s32[1]{0:T(128)} %bitcast.38.len_ref, bf16[1024,512]{1,0:T(8,128)(2,1)S(1)} %add_convert_fusion.4.q_ref, bf16[1024,512]{1,0:T(8,128)(2,1)S(1)} %convolution_convert_fusion.4.k_ref, bf16[1024,512]{1,0:T(8,128)(2,1)S(1)} %add_convert_fusion.3.v_ref), custom_call_target="tpu_custom_call" | custom-call | flops 8589934592 | bytes 4194304 | tf_op jit(solution)/shard_map/pallas_call | solution.py:149
  210.4 7.9 %multiply_convert_fusion = (bf16[1024,2048]{1,0:T(8,128)(2,1)}, f32[1024,2048]{1,0:T(8,128)S(1)}) fusion(f32[2048]{0:T(1024)S(1)} %copy-done.119, bf16[1024,1024]{1,0:T(8,128)(2,1)S(1)} %get-tuple-element.63, bf16[1024,1024]{1,0:T(8,128)(2,1)} %bitcast.71, bf16[1024,1024]{1,0:T(8,128)(2,1)S(1)} %copy-done.89), kind=kOutput, calls=%fused_computation.8 | convolution fusion | flops 4315938816 | bytes 18882560 | tf_op jit(solution)/shard_map/dot_general | solution.py:25
  218.3 8.3 %convert_reduce_fusion = (f32[2048]{0:T(1024)S(1)}, bf16[1024,2048]{1,0:T(8,128)(2,1)S(1)}) fusion(f32[1024,2048]{1,0:T(8,128)S(1)} %get-tuple-element.136, f32[2048]{0:T(1024)S(1)} %copy-done.119, bf16[1024,1024]{1,0:T(8,128)(2,1)} %bitcast.80, bf16[1024,1024]{1,0:T(8,128)(2,1)S(1)} %copy-done.88, bf16[512,1024]{1,0:T(8,128)(2,1)S(1)} %copy-done.61, ...), kind=kOutput, calls=%fused_computation.7 | convolution fusion | flops 4339005440 | bytes 18890752 | tf_op jit(solution)/shard_map/dot_general | solution.py:25
  228.6 8.0 %fusion.135 = (bf16[1024,1024]{1,0:T(8,128)(2,1)}, f32[1024,1024]{1,0:T(8,128)}) fusion(bf16[1024,2048]{1,0:T(8,128)(2,1)S(1)} %get-tuple-element.142, bf16[1024,1024]{1,0:T(8,128)(2,1)} %bitcast.71, bf16[1024,1024]{1,0:T(8,128)(2,1)S(1)} %copy-done.89), kind=kOutput, calls=%fused_computation.370 | convolution fusion | flops 4304404480 | bytes 14680064 | tf_op jit(solution)/shard_map/dot_general | solution.py:25
  236.6 7.8 %reshape.404 = bf16[1024,1,2,1024]{3,2,0,1:T(2,128)(2,1)} reshape(bf16[1024,2048]{1,0:T(8,128)(2,1)} %copy-done.66) | data formatting | bytes 8388608 | tf_op jit(solution)/shard_map/reshape | solution.py:379
  244.4 9.9 %fusion.6 = f32[1024,1024]{1,0:T(8,128)} fusion(bf16[1024,2048]{1,0:T(8,128)(2,1)} %get-tuple-element.135, bf16[1024,1024]{1,0:T(8,128)(2,1)} %bitcast.80, bf16[1024,1024]{1,0:T(8,128)(2,1)} %fusion.162), kind=kOutput, calls=%fused_computation.44 | convolution fusion | flops 4303355904 | bytes 12582912 | tf_op jit(solution)/shard_map/dot_general | solution.py:25
  254.3 8.3 %reshape.408 = bf16[1024,1,2,1024]{3,2,0,1:T(2,128)(2,1)} reshape(bf16[1024,2048]{1,0:T(8,128)(2,1)} %get-tuple-element.135) | data formatting | bytes 8388608 | tf_op jit(solution)/shard_map/reshape | solution.py:379
  264.9 9.9 %fusion.122 = (bf16[1024,1,1,1024]{3,2,0,1:T(2,128)(2,1)}, bf16[1024,1,1,1024]{3,2,0,1:T(2,128)(2,1)S(1)}) fusion(bf16[1024,1,2,1024]{3,2,0,1:T(2,128)(2,1)} %reshape.404), kind=kLoop, calls=%fused_computation.357 | loop fusion | bytes 8388608 | tf_op jit(solution)/shard_map/slice | solution.py:361
  278.7 7.5 collective-permute-start.68
  318.0 27.7 %shard_map.240 = (bf16[1024,512]{1,0:T(8,128)(2,1)S(1)}, bf16[1024,512]{1,0:T(8,128)(2,1)S(1)}, bf16[1024,512]{1,0:T(8,128)(2,1)S(1)}) custom-call(s32[1]{0:T(128)} %bitcast.38.len_ref, bf16[1024,512]{1,0:T(8,128)(2,1)S(1)} %copy-done.12, bf16[1024,512]{1,0:T(8,128)(2,1)S(1)} %copy-done.16, bf16[1024,512]{1,0:T(8,128)(2,1)S(1)} %copy-done.14, ...), custom_call_target="tpu_custom_call" | custom-call | flops 21474836480 | bytes 8388608 | tf_op jit(solution)/shard_map/pallas_call | solution.py:175
  357.7 53.2 %collective-permute-start.38 = (bf16[1024,1024]{1,0:T(8,128)(2,1)}, bf16[1024,1024]{1,0:T(8,128)(2,1)}, u32[]{:S(2)}, u32[]{:S(2)}) collective-permute-start(bf16[1024,1024]{1,0:T(8,128)(2,1)} %get-tuple-element.139), channel_id=1, source_target_pairs={{0,2},{2,0},{4,6},{6,4},{8,10},{10,8},{12,14},{14,12},{16,18},{18,... | collective-permute-start | bytes 6291464 | tf_op jit(solution)/shard_map/ppermute | solution.py:243
  442.2 16.9 %collective-permute-done.48 = bf16[1024,256]{1,0:T(8,128)(2,1)S(1)} collective-permute-done((bf16[1024,256]{1,0:T(8,128)(2,1)S(1)}, bf16[1024,256]{1,0:T(8,128)(2,1)S(1)}, u32[]{:S(2)}, u32[]{:S(2)}) %collective-permute-start.48) | collective-permute-done | bytes 524320 | tf_op jit(solution)/shard_map/ppermute | solution.py:246
  461.9 7.6 collective-permute-done.63
  472.2 16.1 %collective-permute-done.49 = bf16[2,2,2,64,256]{4,3,2,1,0:T(8,128)(2,1)S(1)} collective-permute-done((bf16[2,2,2,64,256]{4,3,2,1,0:T(8,128)(2,1)S(1)}, bf16[2,2,2,64,256]{4,3,2,1,0:T(8,128)(2,1)S(1)}, u32[]{:S(2)}, u32[]{:S(2)}) %collective-permute-start.49) | collective-permute-done | bytes 262176 | tf_op jit(solution)/shard_map/ppermute | solution.py:243
  522.2 15.1 %collective-permute-done.74 = bf16[2,2,2,64,1024]{4,3,2,1,0:T(8,128)(2,1)S(1)} collective-permute-done((bf16[2,2,2,64,1024]{4,3,2,1,0:T(8,128)(2,1)S(1)}, bf16[2,2,2,64,1024]{4,3,2,1,0:T(8,128)(2,1)S(1)}, u32[]{:S(2)}, u32[]{:S(2)}) %collective-permute-start.74) | collective-permute-done | bytes 1048608 | tf_op jit(solution)/shard_map/ppermute | solution.py:243
  547.3 7.8 %collective-permute-done.70 = bf16[2,2,64,1024]{3,2,1,0:T(8,128)(2,1)S(1)} collective-permute-done((bf16[2,2,64,1024]{3,2,1,0:T(8,128)(2,1)S(1)}, bf16[2,2,64,1024]{3,2,1,0:T(8,128)(2,1)S(1)}, u32[]{:S(2)}, u32[]{:S(2)}) %collective-permute-start.70) | collective-permute-done | bytes 524320 | tf_op jit(solution)/shard_map/ppermute | solution.py:243
  590.5 20.3 %shard_map.241 = (bf16[1024,512]{1,0:T(8,128)(2,1)S(1)}, bf16[1024,512]{1,0:T(8,128)(2,1)S(1)}, bf16[1024,512]{1,0:T(8,128)(2,1)S(1)}) custom-call(s32[1]{0:T(128)} %bitcast.2.len_ref, bf16[1024,512]{1,0:T(8,128)(2,1)S(1)} %copy-done.10, bf16[1024,512]{1,0:T(8,128)(2,1)S(1)} %copy-done.6, bf16[1024,512]{1,0:T(8,128)(2,1)S(1)} %copy-done.8, ...), custom_call_target="tpu_custom_call" | custom-call | flops 21474836480 | bytes 8388608 | tf_op jit(solution)/shard_map/pallas_call | solution.py:175
  650.2 41.7 %collective-permute-done.58 = bf16[1024,256]{1,0:T(8,128)(2,1)S(1)} collective-permute-done((bf16[1024,256]{1,0:T(8,128)(2,1)S(1)}, bf16[1024,256]{1,0:T(8,128)(2,1)S(1)}, u32[]{:S(2)}, u32[]{:S(2)}) %collective-permute-start.58) | collective-permute-done | bytes 524320 | tf_op jit(solution)/shard_map/ppermute | solution.py:246
  727.7 15.8 %collective-permute-done.79 = f32[17,1024]{1,0:T(8,128)S(1)} collective-permute-done((f32[17,1024]{1,0:T(8,128)S(1)}, f32[17,1024]{1,0:T(8,128)S(1)}, u32[]{:S(2)}, u32[]{:S(2)}) %collective-permute-start.79) | collective-permute-done | bytes 69664 | tf_op jit(solution)/shard_map/ppermute | solution.py:243
  (655 shorter events, 417.8 us)
Async XLA Ops:
  5.6 69.5 %collective-permute-start = (bf16[512,1024]{1,0:T(8,128)(2,1)}, bf16[512,1024]{1,0:T(8,128)(2,1)S(1)}, u32[]{:S(2)}, u32[]{:S(2)}) collective-permute-start(bf16[512,1024]{1,0:T(8,128)(2,1)} %param.15), channel_id=1, source_target_pairs={{1,2},{2,1},{5,6},{6,5},{9,10},{10,9},{13,14},{14,13},{17,18},{18,... | collective-permute-start | bytes 3145736 | tf_op jit(solution)/shard_map/ppermute | solution.py:252
  84.5 37.5 %collective-permute-start.20 = (bf16[512,1024]{1,0:T(8,128)(2,1)S(1)}, bf16[512,1024]{1,0:T(8,128)(2,1)S(1)}, u32[]{:S(2)}, u32[]{:S(2)}) collective-permute-start(bf16[512,1024]{1,0:T(8,128)(2,1)S(1)} %copy-done.95), channel_id=1, source_target_pairs={{1,2},{2,1},{5,6},{6,5},{9,10},{10,9},{13,14},{14,13},{17,18},{18,... | collective-permute-start | bytes 3145736 | tf_op jit(solution)/shard_map/ppermute | solution.py:252
  85.3 52.7 %collective-permute-start.35 = (bf16[512,1024]{1,0:T(8,128)(2,1)}, bf16[512,1024]{1,0:T(8,128)(2,1)}, u32[]{:S(2)}, u32[]{:S(2)}) collective-permute-start(bf16[512,1024]{1,0:T(8,128)(2,1)} %param.26), channel_id=1, source_target_pairs={{1,2},{2,1},{5,6},{6,5},{9,10},{10,9},{13,14},{14,13},{17,18},{18,... | collective-permute-start | bytes 3145736 | tf_op jit(solution)/shard_map/ppermute | solution.py:252
  133.4 42.8 %collective-permute-start.29 = (bf16[256,1024]{1,0:T(8,128)(2,1)}, bf16[256,1024]{1,0:T(8,128)(2,1)S(1)}, u32[]{:S(2)}, u32[]{:S(2)}) collective-permute-start(bf16[256,1024]{1,0:T(8,128)(2,1)} %collective-permute-done.28), channel_id=1, source_target_pairs={{0,4},{2,6},{4,0},{6,2},{8,12},{10,14},{12,8},{14,10},{16,20},{18,... | collective-permute-start | bytes 1572872 | tf_op jit(solution)/shard_map/ppermute | solution.py:243
  133.4 43.6 %collective-permute-start.27 = (bf16[256,512]{1,0:T(8,128)(2,1)}, bf16[256,512]{1,0:T(8,128)(2,1)}, u32[]{:S(2)}, u32[]{:S(2)}) collective-permute-start(bf16[256,512]{1,0:T(8,128)(2,1)} %slice.284), channel_id=1, source_target_pairs={{0,4},{2,6},{4,0},{6,2},{8,12},{10,14},{12,8},{14,10},{16,20},{18,... | collective-permute-start | bytes 786440 | tf_op jit(solution)/shard_map/ppermute | solution.py:243
  138.0 41.8 %collective-permute-start.26 = (bf16[256,512]{1,0:T(8,128)(2,1)S(1)}, bf16[256,512]{1,0:T(8,128)(2,1)}, u32[]{:S(2)}, u32[]{:S(2)}) collective-permute-start(bf16[256,512]{1,0:T(8,128)(2,1)S(1)} %slice.283), channel_id=1, source_target_pairs={{0,8},{2,10},{4,12},{6,14},{8,0},{10,2},{12,4},{14,6},{16,24},{18,... | collective-permute-start | bytes 786440 | tf_op jit(solution)/shard_map/ppermute | solution.py:243
  141.2 40.4 %collective-permute-start.32 = (bf16[256,512]{1,0:T(8,128)(2,1)}, bf16[256,512]{1,0:T(8,128)(2,1)}, u32[]{:S(2)}, u32[]{:S(2)}) collective-permute-start(bf16[256,512]{1,0:T(8,128)(2,1)} %slice.287), channel_id=1, source_target_pairs={{0,4},{2,6},{4,0},{6,2},{8,12},{10,14},{12,8},{14,10},{16,20},{18,... | collective-permute-start | bytes 786440 | tf_op jit(solution)/shard_map/ppermute | solution.py:243
  145.3 48.3 %collective-permute-start.36 = (bf16[512,1024]{1,0:T(8,128)(2,1)}, bf16[512,1024]{1,0:T(8,128)(2,1)}, u32[]{:S(2)}, u32[]{:S(2)}) collective-permute-start(bf16[512,1024]{1,0:T(8,128)(2,1)} %get-tuple-element.57), channel_id=1, source_target_pairs={{0,2},{2,0},{4,6},{6,4},{8,10},{10,8},{12,14},{14,12},{16,18},{18,... | collective-permute-start | bytes 3145736 | tf_op jit(solution)/shard_map/ppermute | solution.py:243
  264.4 40.1 %collective-permute-start.37 = (bf16[1024,1024]{1,0:T(8,128)(2,1)}, bf16[1024,1024]{1,0:T(8,128)(2,1)}, u32[]{:S(2)}, u32[]{:S(2)}) collective-permute-start(bf16[1024,1024]{1,0:T(8,128)(2,1)} %get-tuple-element.137), channel_id=1, source_target_pairs={{0,2},{2,0},{4,6},{6,4},{8,10},{10,8},{12,14},{14,12},{16,18},{18,... | collective-permute-start | bytes 6291464 | tf_op jit(solution)/shard_map/ppermute | solution.py:243
  278.7 148.9 %collective-permute-start.68 = (bf16[1024,1024]{1,0:T(8,128)(2,1)}, bf16[1024,1024]{1,0:T(8,128)(2,1)}, u32[]{:S(2)}, u32[]{:S(2)}) collective-permute-start(bf16[1024,1024]{1,0:T(8,128)(2,1)} %fusion.18), channel_id=1, source_target_pairs={{0,1},{1,0},{2,3},{3,2},{4,5},{5,4},{6,7},{7,6},{8,9},{9,8},{10,11... | collective-permute-start | bytes 6291464 | tf_op jit(solution)/shard_map/ppermute | solution.py:246
  300.2 133.2 %collective-permute-start.73 = (bf16[1024,1024]{1,0:T(8,128)(2,1)}, bf16[1024,1024]{1,0:T(8,128)(2,1)}, u32[]{:S(2)}, u32[]{:S(2)}) collective-permute-start(bf16[1024,1024]{1,0:T(8,128)(2,1)} %fusion.19), channel_id=1, source_target_pairs={{0,1},{1,0},{2,3},{3,2},{4,5},{5,4},{6,7},{7,6},{8,9},{9,8},{10,11... | collective-permute-start | bytes 6291464 | tf_op jit(solution)/shard_map/ppermute | solution.py:246
  357.7 221.6 %collective-permute-start.38 = (bf16[1024,1024]{1,0:T(8,128)(2,1)}, bf16[1024,1024]{1,0:T(8,128)(2,1)}, u32[]{:S(2)}, u32[]{:S(2)}) collective-permute-start(bf16[1024,1024]{1,0:T(8,128)(2,1)} %get-tuple-element.139), channel_id=1, source_target_pairs={{0,2},{2,0},{4,6},{6,4},{8,10},{10,8},{12,14},{14,12},{16,18},{18,... | collective-permute-start | bytes 6291464 | tf_op jit(solution)/shard_map/ppermute | solution.py:243
  416.1 103.9 %collective-permute-start.41 = (bf16[512,1024]{1,0:T(8,128)(2,1)S(1)}, bf16[512,1024]{1,0:T(8,128)(2,1)S(1)}, u32[]{:S(2)}, u32[]{:S(2)}) collective-permute-start(bf16[512,1024]{1,0:T(8,128)(2,1)S(1)} %fusion.23), channel_id=1, source_target_pairs={{0,2},{2,0},{4,6},{6,4},{8,10},{10,8},{12,14},{14,12},{16,18},{18,... | collective-permute-start | bytes 3145736 | tf_op jit(solution)/shard_map/ppermute | solution.py:243
  421.7 95.6 %collective-permute-start.53 = (bf16[1024,512]{1,0:T(8,128)(2,1)}, bf16[1024,512]{1,0:T(8,128)(2,1)}, u32[]{:S(2)}, u32[]{:S(2)}) collective-permute-start(bf16[1024,512]{1,0:T(8,128)(2,1)} %convolution_convert_fusion.1), channel_id=1, source_target_pairs={{0,1},{1,0},{2,3},{3,2},{4,5},{5,4},{6,7},{7,6},{8,9},{9,8},{10,11... | collective-permute-start | bytes 3145736 | tf_op jit(solution)/shard_map/ppermute | solution.py:246
  433.5 36.0 %collective-permute-start.63 = (bf16[1024,256]{1,0:T(8,128)(2,1)S(1)}, bf16[1024,256]{1,0:T(8,128)(2,1)S(1)}, u32[]{:S(2)}, u32[]{:S(2)}) collective-permute-start(bf16[1024,256]{1,0:T(8,128)(2,1)S(1)} %convolution_convert_fusion.6), channel_id=1, source_target_pairs={{0,1},{1,0},{2,3},{3,2},{4,5},{5,4},{6,7},{7,6},{8,9},{9,8},{10,11... | collective-permute-start | bytes 1572872 | tf_op jit(solution)/shard_map/ppermute | solution.py:246
  459.2 61.9 %collective-permute-start.69 = (bf16[2,2,2,64,1024]{4,3,2,1,0:T(8,128)(2,1)S(1)}, bf16[2,2,2,64,1024]{4,3,2,1,0:T(8,128)(2,1)S(1)}, u32[]{:S(2)}, u32[]{:S(2)}) collective-permute-start(bf16[2,2,2,64,1024]{4,3,2,1,0:T(8,128)(2,1)S(1)} %fusion.24), channel_id=1, source_target_pairs={{0,4},{2,6},{4,0},{6,2},{8,12},{10,14},{12,8},{14,10},{16,20},{18,... | collective-permute-start | bytes 3145736 | tf_op jit(solution)/shard_map/ppermute | solution.py:243
  521.1 56.3 %collective-permute-start.42 = (bf16[512,1024]{1,0:T(8,128)(2,1)S(1)}, bf16[512,1024]{1,0:T(8,128)(2,1)S(1)}, u32[]{:S(2)}, u32[]{:S(2)}) collective-permute-start(bf16[512,1024]{1,0:T(8,128)(2,1)S(1)} %fusion.20), channel_id=1, source_target_pairs={{1,2},{2,1},{5,6},{6,5},{9,10},{10,9},{13,14},{14,13},{17,18},{18,... | collective-permute-start | bytes 3145736 | tf_op jit(solution)/shard_map/ppermute | solution.py:252
  571.8 74.9 %collective-permute-start.72 = (f32[64,1024]{1,0:T(8,128)}, f32[64,1024]{1,0:T(8,128)}, u32[]{:S(2)}, u32[]{:S(2)}) collective-permute-start(f32[64,1024]{1,0:T(8,128)} %dynamic-slice_bitcast_fusion.5), channel_id=1, source_target_pairs={{0,2},{2,0},{4,6},{6,4},{8,10},{10,8},{12,14},{14,12},{16,18},{18,... | collective-permute-start | bytes 786440 | tf_op jit(solution)/shard_map/ppermute | solution.py:243
  576.1 73.0 %collective-permute-start.77 = (f32[64,1024]{1,0:T(8,128)}, f32[64,1024]{1,0:T(8,128)}, u32[]{:S(2)}, u32[]{:S(2)}) collective-permute-start(f32[64,1024]{1,0:T(8,128)} %dynamic-slice_bitcast_fusion.4), channel_id=1, source_target_pairs={{0,2},{2,0},{4,6},{6,4},{8,10},{10,8},{12,14},{14,12},{16,18},{18,... | collective-permute-start | bytes 786440 | tf_op jit(solution)/shard_map/ppermute | solution.py:243
  577.4 53.4 %collective-permute-start.57 = (f32[64,512]{1,0:T(8,128)}, f32[64,512]{1,0:T(8,128)}, u32[]{:S(2)}, u32[]{:S(2)}) collective-permute-start(f32[64,512]{1,0:T(8,128)} %dynamic-slice_bitcast_fusion.8), channel_id=1, source_target_pairs={{0,2},{2,0},{4,6},{6,4},{8,10},{10,8},{12,14},{14,12},{16,18},{18,... | collective-permute-start | bytes 393224 | tf_op jit(solution)/shard_map/ppermute | solution.py:243
  630.8 82.3 %collective-permute-start.39 = (bf16[512,1024]{1,0:T(8,128)(2,1)}, bf16[512,1024]{1,0:T(8,128)(2,1)}, u32[]{:S(2)}, u32[]{:S(2)}) collective-permute-start(bf16[512,1024]{1,0:T(8,128)(2,1)} %fusion.22), channel_id=1, source_target_pairs={{0,2},{2,0},{4,6},{6,4},{8,10},{10,8},{12,14},{14,12},{16,18},{18,... | collective-permute-start | bytes 3145736 | tf_op jit(solution)/shard_map/ppermute | solution.py:243
  641.1 75.7 %collective-permute-start.43 = (bf16[1024,768]{1,0:T(8,128)(2,1)}, bf16[1024,768]{1,0:T(8,128)(2,1)}, u32[]{:S(2)}, u32[]{:S(2)}) collective-permute-start(bf16[1024,768]{1,0:T(8,128)(2,1)} %convolution_convert_fusion), channel_id=1, source_target_pairs={{0,1},{1,0},{2,3},{3,2},{4,5},{5,4},{6,7},{7,6},{8,9},{9,8},{10,11... | collective-permute-start | bytes 4718600 | tf_op jit(solution)/shard_map/ppermute | solution.py:246
  646.2 45.7 %collective-permute-start.58 = (bf16[1024,256]{1,0:T(8,128)(2,1)S(1)}, bf16[1024,256]{1,0:T(8,128)(2,1)S(1)}, u32[]{:S(2)}, u32[]{:S(2)}) collective-permute-start(bf16[1024,256]{1,0:T(8,128)(2,1)S(1)} %convolution_convert_fusion.7), channel_id=1, source_target_pairs={{0,1},{1,0},{2,3},{3,2},{4,5},{5,4},{6,7},{7,6},{8,9},{9,8},{10,11... | collective-permute-start | bytes 1572872 | tf_op jit(solution)/shard_map/ppermute | solution.py:246
  726.0 43.9 %collective-permute-start.40 = (bf16[512,1024]{1,0:T(8,128)(2,1)}, bf16[512,1024]{1,0:T(8,128)(2,1)}, u32[]{:S(2)}, u32[]{:S(2)}) collective-permute-start(bf16[512,1024]{1,0:T(8,128)(2,1)} %get-tuple-element.58), channel_id=1, source_target_pairs={{1,2},{2,1},{5,6},{6,5},{9,10},{10,9},{13,14},{14,13},{17,18},{18,... | collective-permute-start | bytes 3145736 | tf_op jit(solution)/shard_map/ppermute | solution.py:252
  (180 other events, 2154.3 us)
